TPU v7x, 32 devices: a whole 2x2x4 slice. The times are simulated.
32 devices in a mesh: ty: 8 (over y, x, core), tx: 4 (over z).
Axes of the slice: x: 2, y: 2, z: 4, core: 2. Of those that a mesh axis runs over, the one named last changes fastest.
Arguments:
- specimen: float32 [2, 4096, 2048], P(None, 'ty', 'tx'), may hold values from -6 to 6
- probe_field: float32 [2, 256, 256], replicated, may hold values from -6 to 6
- intensity: float32 [256, 256, 256], P(('ty', 'tx')), may hold values from 0.05 to 4
- positions: int32 [256, 2], P(('ty', 'tx')), may hold values from 0 to 3840, as said below
- occupied_slots: int32 [256], P(('ty', 'tx')), may hold values from 0 to 1, as said below
Outputs:
- new_specimen: float32 [2, 4096, 2048], P(None, 'ty', 'tx')
- new_probe: float32 [2, 256, 256], replicated
Inputs may be any that keep to these rules, and one draw needn't show every extreme that they name: `positions`: slots are grouped by tile, 8 to a tile, tiles in the order of ty then tx. A slot of tile (a, b) has its row between a * 512 - 256 // 2 and a * 512 + 512 - 256 // 2 and its column between b * 512 - 256 // 2 and b * 512 + 512 - 256 // 2, and its window lies inside the object. `occupied_slots`: on each tile the live slots come first; each tile has 1 to 8 live slots, and some tile has all 8.
All inputs are finite; a program needn't handle non-finite values.
Results may differ from a plain program's by a relative error of at most 0.0003.
Values sent between devices are 32-bit elements; how exact they have to be, the bound alone decides.
A program may use at most 192 MiB of HBM per device.

v0:
```python
import math

import jax
import jax.numpy as jnp
from jax import lax
from jax.sharding import PartitionSpec as P

ITERS = 2


FLOOR = 0.2
SPECIMEN_REG = 0.5
PROBE_REG = 1.0


def from_behind(value, axis, by):
    length = lax.axis_size(axis)
    pairs = [(i, i + by) for i in range(length) if 0 <= i + by < length]
    return lax.ppermute(value, axis, pairs)


def extended_2(cells, sides, width):
    for axis, dim in sides:
        count = lax.axis_size(axis)
        ends = count - 1
        head = lax.slice_in_dim(cells, 0, width, axis=dim)
        tail = lax.slice_in_dim(cells, cells.shape[dim] - width, cells.shape[dim], axis=dim)
        cells = jnp.concatenate(
            [
                lax.ppermute(tail, axis, [(i, (i + 1) % count) for i in range(ends)]),
                cells,
                lax.ppermute(head, axis, [((i + 1) % count, i) for i in range(ends)]),
            ],
            axis=dim,
        )
    return cells


def dft_tables(window):
    indices = jnp.arange(window, dtype=jnp.int32)
    products = indices[:, None] * indices[None, :] % window
    angles = products.astype(jnp.float32) * (2.0 * math.pi / window)
    norm_scale = 1.0 / math.sqrt(window)
    return (jnp.cos(angles) * norm_scale, jnp.sin(angles) * norm_scale)


def apply_left(matrix, batch):
    return jnp.einsum("jk,pkl->pjl", matrix, batch, precision=lax.Precision.HIGHEST)


def apply_right(batch, matrix):
    return jnp.einsum("pjk,kl->pjl", batch, matrix, precision=lax.Precision.HIGHEST)


def transform(in_real, in_imag, cosine_table, sine_table, direction_sign):
    half_real = apply_left(cosine_table, in_real) - direction_sign * apply_left(sine_table, in_imag)
    half_imag = apply_left(cosine_table, in_imag) + direction_sign * apply_left(sine_table, in_real)
    out_real = apply_right(half_real, cosine_table) - direction_sign * apply_right(
        half_imag, sine_table
    )
    out_imag = apply_right(half_imag, cosine_table) + direction_sign * apply_right(
        half_real, sine_table
    )
    return (out_real, out_imag)


def run_slots(
    extended, probe_field, corners, measured_amplitude, alive, cosine_table, sine_table, state_tuple
):
    totals, probe_grad, probe_density = state_tuple
    window = probe_field.shape[1]
    anchor = jnp.zeros((), jnp.int32)
    patches = jax.vmap(
        lambda corner: lax.dynamic_slice(
            extended, (anchor, corner[0], corner[1]), (2, window, window)
        )
    )(corners)
    patch_real = patches[:, 0]
    patch_imag = patches[:, 1]
    probe_real = probe_field[0]
    probe_imag = probe_field[1]
    exit_real = probe_real * patch_real - probe_imag * patch_imag
    exit_imag = probe_real * patch_imag + probe_imag * patch_real
    spectrum_real, spectrum_imag = transform(exit_real, exit_imag, cosine_table, sine_table, -1.0)
    magnitude = jnp.sqrt(spectrum_real * spectrum_real + spectrum_imag * spectrum_imag)
    factor = measured_amplitude / jnp.maximum(magnitude, FLOOR)
    back_real, back_imag = transform(
        spectrum_real * factor, spectrum_imag * factor, cosine_table, sine_table, 1.0
    )
    weight_live = alive[:, None, None]
    diff_real = weight_live * (back_real - exit_real)
    diff_imag = weight_live * (back_imag - exit_imag)
    contribution = jnp.stack(
        [
            probe_real * diff_real + probe_imag * diff_imag,
            probe_real * diff_imag - probe_imag * diff_real,
            weight_live * (probe_real * probe_real + probe_imag * probe_imag),
        ],
        axis=1,
    )
    probe_grad = jnp.stack(
        [
            jnp.sum(patch_real * diff_real + patch_imag * diff_imag, axis=0),
            jnp.sum(patch_real * diff_imag - patch_imag * diff_real, axis=0),
        ]
    )
    probe_density = jnp.sum(
        weight_live * (patch_real * patch_real + patch_imag * patch_imag), axis=0
    )

    def deposit(slot, running):
        start_row = corners[slot, 0]
        start_col = corners[slot, 1]
        region = lax.dynamic_slice(running, (anchor, start_row, start_col), (3, window, window))
        return lax.dynamic_update_slice(
            running, region + contribution[slot], (anchor, start_row, start_col)
        )

    totals = lax.fori_loop(0, corners.shape[0], deposit, totals)
    return (totals, probe_grad, probe_density)


def fold_columns(totals, margin):
    span_cells = totals.shape[2] - 2 * margin
    interior = totals[:, :, margin : margin + span_cells]
    for direction in (1, -1):
        outgoing = totals[:, :, margin + span_cells :] if direction == 1 else totals[:, :, :margin]
        incoming = from_behind(outgoing, "tx", direction)
        if direction == 1:
            interior = interior.at[:, :, :margin].add(incoming)
        else:
            interior = interior.at[:, :, span_cells - margin :].add(incoming)
    return interior


def fold_rows(totals, margin):
    span_cells = totals.shape[1] - 2 * margin
    interior = totals[:, margin : margin + span_cells, :]
    for direction in (1, -1):
        outgoing = totals[:, margin + span_cells :, :] if direction == 1 else totals[:, :margin, :]
        incoming = from_behind(outgoing, "ty", direction)
        if direction == 1:
            interior = interior.at[:, :margin, :].add(incoming)
        else:
            interior = interior.at[:, span_cells - margin :, :].add(incoming)
    return interior


def body(specimen, probe_field, intensity, positions, occupied_slots):
    tile_rows = specimen.shape[1]
    tile_columns = specimen.shape[2]
    window = probe_field.shape[1]
    margin = window // 2
    row_start = lax.axis_index("ty") * tile_rows - margin
    column_start = lax.axis_index("tx") * tile_columns - margin
    local_corner = positions - jnp.stack([row_start, column_start])[None, :]
    measured_amplitude = jnp.sqrt(intensity)
    alive = occupied_slots.astype(jnp.float32)
    cosine_table, sine_table = dft_tables(window)
    for iteration in range(ITERS):
        extended = extended_2(specimen, (("ty", 1), ("tx", 2)), margin)
        starting_state = (
            jnp.zeros((3, extended.shape[1], extended.shape[2]), jnp.float32),
            jnp.zeros((2, window, window), jnp.float32),
            jnp.zeros((window, window), jnp.float32),
        )
        totals, probe_grad, probe_density = run_slots(
            extended,
            probe_field,
            local_corner,
            measured_amplitude,
            alive,
            cosine_table,
            sine_table,
            starting_state,
        )
        interior = fold_rows(fold_columns(totals, margin), margin)
        new_specimen = specimen + interior[:2] / (interior[2] + SPECIMEN_REG)
        grad_total, density_total = lax.psum((probe_grad, probe_density), ("ty", "tx"))
        probe_field = probe_field + grad_total / (density_total + PROBE_REG)
        specimen = new_specimen
    return (specimen, probe_field)


def solution(mesh):
    return jax.shard_map(
        body,
        mesh=mesh,
        in_specs=(
            P(None, "ty", "tx"),
            P(),
            P(("ty", "tx"), None, None),
            P(("ty", "tx"), None),
            P(("ty", "tx")),
        ),
        out_specs=(P(None, "ty", "tx"), P()),
        check_vma=False,
    )
```

profile of v0, /device:TPU:0, one launch (start us, length us, event | category | flops | bytes accessed | tf_op | source)
XLA Modules:
  0.0 944.2 jit_solution(8598801132877512158)
XLA Ops:
  40.7 33.1 %while.38 = (s32[]{:T(128)}, f32[2,768,768]{2,1,0:T(8,128)}, s32[8,3]{0,1:T(4,128)S(1)}, f32[8,2,256,256]{3,2,0,1:T(8,128)}, s32[]{:T(128)}) while((s32[]{:T(128)}, f32[2,768,768]{2,1,0:T(8,128)}, s32[8,3]{0,1:T(4,128)S(1)}, f32[8,2,256,256]{3,2,0,1:T(8,128)}, s32[]{:T(128)}) %tuple.151), condition=%wide.while_cond.8, body=%wide.while_body.8.sunk | while | flops 2 | bytes 1050217 | solution.py:74
  146.6 9.1 fusion.46
  156.7 145.0 %all-reduce.7.cloned.1.call-done = (f32[2,256,256]{2,1,0:T(8,128)}, f32[256,256]{1,0:T(8,128)}) async-done(((f32[2,256,256]{2,1,0:T(8,128)}, f32[256,256]{1,0:T(8,128)}), (f32[2,256,256]{2,1,0:T(8,128)}, f32[256,256]{1,0:T(8,128)})) %all-reduce.7.cloned.1.call-update) | async-done | bytes 786448 | tf_op jit(solution)/shard_map/psum | solution.py:179
  312.8 120.2 %while.36 = (s32[]{:T(128)}, f32[3,768,768]{2,1,0:T(8,128)}, s32[8,2]{0,1:T(2,128)S(1)}, f32[8,3,256,256]{3,2,0,1:T(8,128)}, s32[]{:T(128)}, /*index=5*/s32[]{:T(128)}, s32[]{:T(128)}) while((s32[]{:T(128)}, f32[3,768,768]{2,1,0:T(8,128)}, s32[8,2]{0,1:T(2,128)S(1)}, f32[8,3,256,256]{3,2,0,1:T(8,128)}, s32[]{:T(128)}, /*index=5*/s32[]{:T(128)}, ...), condition=%wide.region_1.2_spmd, body=%wide.region_0.1_spmd.sunk | while | flops 196616 | bytes 3932341 | solution.py:119
  319.1 8.3 dynamic_update_slice.16
  348.2 9.2 dynamic_update_slice.16
  363.7 8.3 dynamic_update_slice.16
  378.3 9.5 %dynamic_update_slice.16 = f32[3,768,768]{2,1,0:T(8,128)} dynamic-update-slice(f32[3,768,768]{2,1,0:T(8,128)} %get-tuple-element.513, f32[3,256,256]{2,1,0:T(8,128)S(1)} %bitcast_add_fusion.4, s32[]{:T(128)} %constant.274.clone.1..sunk, s32[]{:T(128)S(6)} %select_n.247, s32[]{:T(128)S(6)} %select_n.248) | dynamic-update-slice | bytes 1572868 | tf_op jit(solution)/shard_map/while/body/eval_jaxpr/dynamic_update_slice | solution.py:115
  394.1 9.1 dynamic_update_slice.16
  409.6 8.3 dynamic_update_slice.16
  424.2 8.8 dynamic_update_slice.16
  446.2 18.5 %collective-permute-done.4 = f32[3,768,128]{2,1,0:T(8,128)S(1)} collective-permute-done((f32[3,768,128]{2,1,0:T(8,128)S(1)}, f32[3,768,128]{2,1,0:T(8,128)S(1)}, u32[]{:S(2)}, u32[]{:S(2)}) %collective-permute-start.4) | collective-permute-done | bytes 1179680 | tf_op jit(solution)/shard_map/ppermute | solution.py:19
  479.6 17.2 %collective-permute-start.8 = (f32[2,128,512]{2,1,0:T(8,128)S(1)}, f32[2,128,512]{2,1,0:T(8,128)S(1)}, u32[]{:S(2)}, u32[]{:S(2)}) collective-permute-start(f32[2,128,512]{2,1,0:T(8,128)S(1)} %get-tuple-element.360), channel_id=1, source_target_pairs={{0,4},{4,8},{8,12},{12,16},{16,20},{20,24},{24,28},{1,5},{5,9},{9,... | collective-permute-start | bytes 1572872 | tf_op jit(solution)/shard_map/ppermute | solution.py:30
  525.1 32.8 %while.39 = (s32[]{:T(128)}, f32[2,768,768]{2,1,0:T(8,128)}, s32[8,3]{0,1:T(4,128)S(1)}, f32[8,2,256,256]{3,2,0,1:T(8,128)}, s32[]{:T(128)}) while((s32[]{:T(128)}, f32[2,768,768]{2,1,0:T(8,128)}, s32[8,3]{0,1:T(4,128)S(1)}, f32[8,2,256,256]{3,2,0,1:T(8,128)}, s32[]{:T(128)}) %tuple.169), condition=%wide.while_cond.9, body=%wide.while_body.9.sunk | while | flops 2 | bytes 1050217 | solution.py:74
  644.9 120.3 %while.37 = (s32[]{:T(128)}, f32[3,768,768]{2,1,0:T(8,128)}, s32[8,2]{0,1:T(2,128)S(1)}, f32[8,3,256,256]{3,2,0,1:T(8,128)}, s32[]{:T(128)}, /*index=5*/s32[]{:T(128)}, s32[]{:T(128)}) while((s32[]{:T(128)}, f32[3,768,768]{2,1,0:T(8,128)}, s32[8,2]{0,1:T(2,128)S(1)}, f32[8,3,256,256]{3,2,0,1:T(8,128)}, s32[]{:T(128)}, /*index=5*/s32[]{:T(128)}, ...), condition=%wide.region_8.9_spmd, body=%wide.region_7.8_spmd.sunk | while | flops 196616 | bytes 3932341 | solution.py:119
  651.2 8.3 dynamic_update_slice.17
  680.3 9.2 dynamic_update_slice.17
  710.5 9.5 %dynamic_update_slice.17 = f32[3,768,768]{2,1,0:T(8,128)} dynamic-update-slice(f32[3,768,768]{2,1,0:T(8,128)} %get-tuple-element.549, f32[3,256,256]{2,1,0:T(8,128)S(1)} %bitcast_add_fusion.5, s32[]{:T(128)} %constant.274.clone.1..sunk.1, s32[]{:T(128)S(6)} %select_n.249, s32[]{:T(128)S(6)} %select_n.250) | dynamic-update-slice | bytes 1572868 | tf_op jit(solution)/shard_map/while/body/eval_jaxpr/dynamic_update_slice | solution.py:115
  726.3 9.1 dynamic_update_slice.17
  741.8 8.3 dynamic_update_slice.17
  756.4 8.8 dynamic_update_slice.17
  782.0 10.8 %collective-permute-done.12 = f32[3,768,128]{2,1,0:T(8,128)} collective-permute-done((f32[3,768,128]{2,1,0:T(8,128)}, f32[3,768,128]{2,1,0:T(8,128)}, u32[]{:S(2)}, u32[]{:S(2)}) %collective-permute-start.12) | collective-permute-done | bytes 1179680 | tf_op jit(solution)/shard_map/ppermute | solution.py:19
  804.3 10.4 %collective-permute-start.14 = (f32[3,128,512]{2,1,0:T(8,128)}, f32[3,128,512]{2,1,0:T(8,128)}, u32[]{:S(2)}, u32[]{:S(2)}) collective-permute-start(f32[3,128,512]{2,1,0:T(8,128)} %get-tuple-element.341), channel_id=1, source_target_pairs={{0,4},{4,8},{8,12},{12,16},{16,20},{20,24},{24,28},{1,5},{5,9},{9,... | collective-permute-start | bytes 2359304 | tf_op jit(solution)/shard_map/ppermute | solution.py:19
  816.0 111.1 %all-reduce.5.cloned.1.call-done = (f32[2,256,256]{2,1,0:T(8,128)}, f32[256,256]{1,0:T(8,128)}) async-done(((f32[2,256,256]{2,1,0:T(8,128)}, f32[256,256]{1,0:T(8,128)}), (f32[2,256,256]{2,1,0:T(8,128)}, f32[256,256]{1,0:T(8,128)})) %all-reduce.5.cloned.1.call-update) | async-done | bytes 786448 | tf_op jit(solution)/shard_map/psum | solution.py:179
  (230 shorter events, 429.8 us)
Async XLA Ops:
  7.2 6.6 copy-start.2
  7.2 294.5 %all-reduce.7.cloned.1.call-start = ((), (), s32[]{:S(2)}) async-start(), calls=%async_computation.1 | async-start | bytes 1572864 | tf_op jit(solution)/shard_map/psum | solution.py:179
  9.6 4.1 collective-permute-start
  12.0 6.1 collective-permute-start.1
  13.9 9.2 copy-start.12
  13.9 9.2 copy-start.8
  18.2 13.0 %collective-permute-start.2 = (f32[2,768,128]{2,1,0:T(8,128)S(1)}, f32[2,768,128]{2,1,0:T(8,128)S(1)}, u32[]{:S(2)}, u32[]{:S(2)}) collective-permute-start(f32[2,768,128]{2,1,0:T(8,128)S(1)} %get-tuple-element.358), channel_id=1, source_target_pairs={{0,1},{1,2},{2,3},{4,5},{5,6},{6,7},{8,9},{9,10},{10,11},{12,13},{... | collective-permute-start | bytes 2359304 | tf_op jit(solution)/shard_map/ppermute | solution.py:30
  21.8 13.9 %collective-permute-start.3 = (f32[2,768,128]{2,1,0:T(8,128)S(1)}, f32[2,768,128]{2,1,0:T(8,128)S(1)}, u32[]{:S(2)}, u32[]{:S(2)}) collective-permute-start(f32[2,768,128]{2,1,0:T(8,128)S(1)} %get-tuple-element.359), channel_id=1, source_target_pairs={{1,0},{2,1},{3,2},{5,4},{6,5},{7,6},{9,8},{10,9},{11,10},{13,12},{... | collective-permute-start | bytes 2359304 | tf_op jit(solution)/shard_map/ppermute | solution.py:32
  155.8 146.9 %copy-start.9 = (f32[2,256,256]{2,1,0:T(8,128)S(1)}, f32[2,256,256]{2,1,0:T(8,128)}, u32[]{:S(2)}) copy-start(f32[2,256,256]{2,1,0:T(8,128)} %param.26) | copy-start | bytes 1572868
  156.6 770.5 %all-reduce.5.cloned.1.call-start = ((), (), s32[]{:S(2)}) async-start(), calls=%async_computation | async-start | bytes 1572864 | tf_op jit(solution)/shard_map/psum | solution.py:179
  434.8 29.9 %collective-permute-start.4 = (f32[3,768,128]{2,1,0:T(8,128)S(1)}, f32[3,768,128]{2,1,0:T(8,128)S(1)}, u32[]{:S(2)}, u32[]{:S(2)}) collective-permute-start(f32[3,768,128]{2,1,0:T(8,128)S(1)} %get-tuple-element.335), channel_id=1, source_target_pairs={{0,1},{1,2},{2,3},{4,5},{5,6},{6,7},{8,9},{9,10},{10,11},{12,13},{... | collective-permute-start | bytes 3538952 | tf_op jit(solution)/shard_map/ppermute | solution.py:19
  442.0 27.4 %collective-permute-start.5 = (f32[3,768,128]{2,1,0:T(8,128)S(1)}, f32[3,768,128]{2,1,0:T(8,128)S(1)}, u32[]{:S(2)}, u32[]{:S(2)}) collective-permute-start(f32[3,768,128]{2,1,0:T(8,128)S(1)} %get-tuple-element.334), channel_id=1, source_target_pairs={{1,0},{2,1},{3,2},{5,4},{6,5},{7,6},{9,8},{10,9},{11,10},{13,12},{... | collective-permute-start | bytes 3538952 | tf_op jit(solution)/shard_map/ppermute | solution.py:19
  469.8 3.2 collective-permute-start.6
  471.2 7.4 collective-permute-start.7
  479.6 18.6 %collective-permute-start.8 = (f32[2,128,512]{2,1,0:T(8,128)S(1)}, f32[2,128,512]{2,1,0:T(8,128)S(1)}, u32[]{:S(2)}, u32[]{:S(2)}) collective-permute-start(f32[2,128,512]{2,1,0:T(8,128)S(1)} %get-tuple-element.360), channel_id=1, source_target_pairs={{0,4},{4,8},{8,12},{12,16},{16,20},{20,24},{24,28},{1,5},{5,9},{9,... | collective-permute-start | bytes 1572872 | tf_op jit(solution)/shard_map/ppermute | solution.py:30
  496.7 3.8 collective-permute-start.9
  501.9 11.9 %collective-permute-start.10 = (f32[2,768,128]{2,1,0:T(8,128)}, f32[2,768,128]{2,1,0:T(8,128)}, u32[]{:S(2)}, u32[]{:S(2)}) collective-permute-start(f32[2,768,128]{2,1,0:T(8,128)} %get-tuple-element.356), channel_id=1, source_target_pairs={{0,1},{1,2},{2,3},{4,5},{5,6},{6,7},{8,9},{9,10},{10,11},{12,13},{... | collective-permute-start | bytes 2359304 | tf_op jit(solution)/shard_map/ppermute | solution.py:30
  504.9 14.2 %collective-permute-start.11 = (f32[2,768,128]{2,1,0:T(8,128)}, f32[2,768,128]{2,1,0:T(8,128)}, u32[]{:S(2)}, u32[]{:S(2)}) collective-permute-start(f32[2,768,128]{2,1,0:T(8,128)} %get-tuple-element.357), channel_id=1, source_target_pairs={{1,0},{2,1},{3,2},{5,4},{6,5},{7,6},{9,8},{10,9},{11,10},{13,12},{... | collective-permute-start | bytes 2359304 | tf_op jit(solution)/shard_map/ppermute | solution.py:32
  631.0 7.4 copy-start.4
  768.4 24.3 %collective-permute-start.12 = (f32[3,768,128]{2,1,0:T(8,128)}, f32[3,768,128]{2,1,0:T(8,128)}, u32[]{:S(2)}, u32[]{:S(2)}) collective-permute-start(f32[3,768,128]{2,1,0:T(8,128)} %get-tuple-element.333), channel_id=1, source_target_pairs={{0,1},{1,2},{2,3},{4,5},{5,6},{6,7},{8,9},{9,10},{10,11},{12,13},{... | collective-permute-start | bytes 3538952 | tf_op jit(solution)/shard_map/ppermute | solution.py:19
  774.7 6.4 copy-start.11
  774.7 23.9 %collective-permute-start.13 = (f32[3,768,128]{2,1,0:T(8,128)}, f32[3,768,128]{2,1,0:T(8,128)}, u32[]{:S(2)}, u32[]{:S(2)}) collective-permute-start(f32[3,768,128]{2,1,0:T(8,128)} %get-tuple-element.332), channel_id=1, source_target_pairs={{1,0},{2,1},{3,2},{5,4},{6,5},{7,6},{9,8},{10,9},{11,10},{13,12},{... | collective-permute-start | bytes 3538952 | tf_op jit(solution)/shard_map/ppermute | solution.py:19
  804.3 128.0 %collective-permute-start.14 = (f32[3,128,512]{2,1,0:T(8,128)}, f32[3,128,512]{2,1,0:T(8,128)}, u32[]{:S(2)}, u32[]{:S(2)}) collective-permute-start(f32[3,128,512]{2,1,0:T(8,128)} %get-tuple-element.341), channel_id=1, source_target_pairs={{0,4},{4,8},{8,12},{12,16},{16,20},{20,24},{24,28},{1,5},{5,9},{9,... | collective-permute-start | bytes 2359304 | tf_op jit(solution)/shard_map/ppermute | solution.py:19
  814.7 119.0 %collective-permute-start.15 = (f32[3,128,512]{2,1,0:T(8,128)}, f32[3,128,512]{2,1,0:T(8,128)}, u32[]{:S(2)}, u32[]{:S(2)}) collective-permute-start(f32[3,128,512]{2,1,0:T(8,128)} %get-tuple-element.340), channel_id=1, source_target_pairs={{4,0},{8,4},{12,8},{16,12},{20,16},{24,20},{28,24},{5,1},{9,5},{13... | collective-permute-start | bytes 2359304 | tf_op jit(solution)/shard_map/ppermute | solution.py:19
  (10 other events, 44.6 us)
Sparse Core Ops, SparseCore 0:
  156.7 144.9 all-reduce.6
  782.1 144.9 all-reduce.4
where the time goes:
time: 954 us; the launch traced here: 944 us
  waiting for transfers between devices  330 us (35%)
  local copies, waits for them, and re-layouts  248 us (26%)
  matrix products  157 us (16%)
  other arithmetic  70.6 us (7%)
  loops' own time  62.5 us (7%)
  starting transfers between devices  61.9 us (6%)
  between operations  14.9 us (2%)
    psum x2, waiting for transfers between devices, body(): lax.psum((probe_grad, probe_density), ('ty', 'tx'))  256 us
    dynamic_update_slice x16, local copies, waits for them, and re-layouts, deposit(): lax.dynamic_update_slice(running, region + contribution[slot], (anchor, s...  139 us
    dot_general x16, matrix products, apply_right(): jnp.einsum('pjk,kl->pjl', batch, matrix, precision=lax.Precision.HIGHEST)  83.8 us
    dot_general x16, matrix products, apply_left(): jnp.einsum('jk,pkl->pjl', matrix, batch, precision=lax.Precision.HIGHEST)  73 us
    gather x48, local copies, waits for them, and re-layouts  65.2 us
    another operation x2, loops' own time, run_slots(): totals = lax.fori_loop(0, corners.shape[0], deposit, totals)  61.8 us
    ppermute x8, waiting for transfers between devices, from_behind(): return lax.ppermute(value, axis, pairs)  41.2 us
    ppermute x8, starting transfers between devices, from_behind(): return lax.ppermute(value, axis, pairs)  30.6 us
  transfers between devices with their start and end apart: 18, of which 16 were waited for; matrix products, arithmetic and copies ran while one was open for 3% of the time, Pallas kernels for 0%

commit v1 on v0

v1 whole, which is shorter than its diff:
```python
import functools
import math

import jax
import jax.numpy as jnp
import ml_dtypes
import numpy as np
from jax import lax
from jax.experimental import pallas as pl
from jax.experimental.pallas import tpu as pltpu
from jax.sharding import PartitionSpec as P

ITERS = 2


FLOOR = 0.2
SPECIMEN_REG = 0.5
PROBE_REG = 1.0
LANES = 128
SUBLANES = 8


def split_np(table):
    hi = table.astype(ml_dtypes.bfloat16)
    lo = (table - hi.astype(np.float64)).astype(ml_dtypes.bfloat16)
    return hi, lo


def tables(window):
    half = window // 2
    j = np.arange(half)[:, None]
    m = np.arange(window)[None, :]
    angle = 2.0 * math.pi * ((j * m) % window) / window
    lower = np.sin(angle)
    lower[0] = np.cos(math.pi * m[0])
    real_dft = np.concatenate([np.cos(angle), lower]) / math.sqrt(window)
    hi, lo = split_np(real_dft)
    wide = np.concatenate([hi, hi, lo], axis=1)
    hi_t, lo_t = hi.T.copy(), lo.T.copy()
    wide_t = np.concatenate([hi_t, hi_t, lo_t], axis=1)
    order = np.concatenate([np.arange(half + 1), np.arange(window - 1, half, -1)])
    perm = np.zeros((window, window), ml_dtypes.bfloat16)
    perm[np.arange(window), order] = 1
    return (
        wide,
        wide.T.copy(),
        wide_t,
        wide_t.T.copy(),
        perm,
        perm.T.copy(),
    )


def dot(a, b):
    return jnp.dot(a, b, preferred_element_type=jnp.float32)


def split(x):
    hi = x.astype(jnp.bfloat16)
    return hi, (x - hi.astype(jnp.float32)).astype(jnp.bfloat16)


def times_left(wide, x):
    hi, lo = split(x)
    return dot(wide, jnp.concatenate([hi, lo, hi], axis=0))


def times_right(x, wide):
    hi, lo = split(x)
    return dot(jnp.concatenate([hi, lo, hi], axis=1), wide)


def halves(x, axis):
    half = x.shape[axis] // 2
    return (x[:half], x[half:]) if axis == 0 else (x[:, :half], x[:, half:])


def spread(ur, ui, axis):
    ar, br = halves(ur, axis)
    ai, bi = halves(ui, axis)
    first = lax.broadcasted_iota(jnp.int32, ar.shape, axis) == 0
    yr = jnp.concatenate(
        [ar + jnp.where(first, 0.0, bi), jnp.where(first, br, ar - bi)], axis=axis
    )
    yi = jnp.concatenate(
        [ai - jnp.where(first, 0.0, br), jnp.where(first, bi, ai + br)], axis=axis
    )
    return yr, yi


def gather_pairs(zr, zi, axis):
    ar, br = halves(zr, axis)
    ai, bi = halves(zi, axis)
    first = lax.broadcasted_iota(jnp.int32, ar.shape, axis) == 0
    xr = jnp.concatenate(
        [ar + jnp.where(first, 0.0, br), jnp.where(first, br, bi - ai)], axis=axis
    )
    xi = jnp.concatenate(
        [ai + jnp.where(first, 0.0, bi), jnp.where(first, bi, ar - br)], axis=axis
    )
    return xr, xi


def sweep_kernel(
    corner_ref, alive_ref, ext_ref, probe_ref, intensity_ref,
    left_ref, right_ref, left_t_ref, right_t_ref, perm_ref, perm_t_ref,
    totals_ref, grad_ref, power_ref,
):
    window = probe_ref.shape[1]
    slots = intensity_ref.shape[0]
    last_top = ext_ref.shape[1] - window - SUBLANES
    last_start = ext_ref.shape[2] - window - LANES
    totals_ref[...] = jnp.zeros_like(totals_ref)
    grad_ref[...] = jnp.zeros_like(grad_ref)
    power_ref[...] = probe_ref[0] * probe_ref[0] + probe_ref[1] * probe_ref[1]
    lane = lax.broadcasted_iota(jnp.int32, (window + SUBLANES, LANES), 1)
    pieces = (window // SUBLANES, SUBLANES, LANES)
    sublane = lax.broadcasted_iota(jnp.int32, pieces, 1)
    sublane_tall = lax.broadcasted_iota(jnp.int32, (pieces[0] + 1, *pieces[1:]), 1)

    def visit(slot, carry):
        @pl.when(alive_ref[slot] != 0)
        def _():
            row = corner_ref[slot, 0]
            column = corner_ref[slot, 1]
            top = jnp.minimum((row // SUBLANES) * SUBLANES, last_top)
            down = row - top
            top = pl.multiple_of(top, SUBLANES)
            start = jnp.minimum((column // LANES) * LANES, last_start)
            shift = column - start
            start = pl.multiple_of(start, LANES)
            weight = alive_ref[slot].astype(jnp.float32)
            count = window // LANES
            tall = window + SUBLANES
            groups = window // SUBLANES

            def strip(plane, j):
                return (plane, pl.ds(top, tall), pl.ds(start + j * LANES, LANES))

            def fetch(plane):
                blocks = [
                    pltpu.roll(ext_ref[strip(plane, j)], lax.rem(LANES - shift, LANES), 1)
                    for j in range(count + 1)
                ]
                out = []
                for j in range(count):
                    block = jnp.where(lane < LANES - shift, blocks[j], blocks[j + 1])
                    block = block.reshape(groups + 1, SUBLANES, LANES)
                    block = pltpu.roll(block, lax.rem(SUBLANES - down, SUBLANES), 1)
                    block = jnp.where(sublane < SUBLANES - down, block[:-1], block[1:])
                    out.append(block.reshape(window, LANES))
                return jnp.concatenate(out, axis=1)

            def deposit(plane, value):
                blocks = []
                none = jnp.zeros((1, SUBLANES, LANES), jnp.float32)
                for j in range(count):
                    block = value[:, j * LANES : (j + 1) * LANES]
                    block = block.reshape(groups, SUBLANES, LANES)
                    block = pltpu.roll(block, lax.rem(down, SUBLANES), 1)
                    here = jnp.concatenate([block, none], axis=0)
                    before = jnp.concatenate([none, block], axis=0)
                    block = jnp.where(sublane_tall >= down, here, before)
                    blocks.append(pltpu.roll(block.reshape(tall, LANES), lax.rem(shift, LANES), 1))
                for j in range(count + 1):
                    here = blocks[j] if j < count else jnp.zeros_like(blocks[0])
                    before = blocks[j - 1] if j > 0 else jnp.zeros_like(blocks[0])
                    totals_ref[strip(plane, j)] += jnp.where(lane >= shift, here, before)

            patch_r, patch_i = fetch(0), fetch(1)
            probe_r, probe_i = probe_ref[0], probe_ref[1]
            exit_r = probe_r * patch_r - probe_i * patch_i
            exit_i = probe_r * patch_i + probe_i * patch_r
            yr, yi = spread(
                times_left(left_ref[...], exit_r), times_left(left_ref[...], exit_i), 0
            )
            zr, zi = spread(
                times_right(yr, right_ref[...]), times_right(yi, right_ref[...]), 1
            )
            amplitude = jnp.sqrt(intensity_ref[slot])
            hi, mid = split(amplitude)
            rest = amplitude - hi.astype(jnp.float32) - mid.astype(jnp.float32)
            low = rest.astype(jnp.bfloat16)
            rows = [dot(perm_ref[...], part).astype(jnp.bfloat16) for part in (hi, mid, low)]
            amplitude = sum(dot(part, perm_t_ref[...]) for part in rows)
            magnitude = jnp.sqrt(zr * zr + zi * zi)
            factor = amplitude / jnp.maximum(magnitude, FLOOR)
            zr, zi = gather_pairs(zr * factor, zi * factor, 0)
            yr, yi = times_left(left_t_ref[...], zr), times_left(left_t_ref[...], zi)
            yr, yi = gather_pairs(yr, yi, 1)
            back_r, back_i = times_right(yr, right_t_ref[...]), times_right(yi, right_t_ref[...])
            diff_r = weight * (back_r - exit_r)
            diff_i = weight * (back_i - exit_i)
            deposit(0, probe_r * diff_r + probe_i * diff_i)
            deposit(1, probe_r * diff_i - probe_i * diff_r)
            deposit(2, weight * power_ref[...])
            grad_ref[0] += patch_r * diff_r + patch_i * diff_i
            grad_ref[1] += patch_r * diff_i - patch_i * diff_r
            grad_ref[2] += weight * (patch_r * patch_r + patch_i * patch_i)

        return carry

    lax.fori_loop(0, slots, visit, 0)


def sweep(corners, occupied, extended, probe_field, intensity):
    window = probe_field.shape[1]
    rows, columns = extended.shape[1:]
    smem = pl.BlockSpec(memory_space=pltpu.SMEM)
    vmem = pl.BlockSpec(memory_space=pltpu.VMEM)
    consts = [jnp.asarray(t) for t in tables(window)]
    return pl.pallas_call(
        sweep_kernel,
        out_shape=(
            jax.ShapeDtypeStruct((3, rows, columns), jnp.float32),
            jax.ShapeDtypeStruct((3, window, window), jnp.float32),
        ),
        in_specs=[smem, smem] + [vmem] * (3 + len(consts)),
        out_specs=(vmem, vmem),
        scratch_shapes=[pltpu.VMEM((window, window), jnp.float32)],
        compiler_params=pltpu.CompilerParams(vmem_limit_bytes=48 * 1024 * 1024),
        name="sweep",
    )(corners, occupied, extended, probe_field, intensity, *consts)


class Shift:
    def __init__(self, net, src, dst, axis, delta, also=None):
        self.net, self.src, self.dst = net, src, dst
        self.slot = net.slot()
        here, count = net.place[axis], net.size[axis]
        self.sends = here + delta < count if delta > 0 else here > 0
        self.gets = here > 0 if delta > 0 else here - delta < count
        if also is not None:
            self.sends = jnp.logical_and(self.sends, also)
            self.gets = jnp.logical_and(self.gets, also)
        self.target = net.target(axis, here + delta)

    def copy(self):
        return pltpu.make_async_remote_copy(
            src_ref=self.src,
            dst_ref=self.dst,
            send_sem=self.net.send_sem.at[self.slot],
            recv_sem=self.net.recv_sem.at[self.slot],
            device_id=self.target,
            device_id_type=pl.DeviceIdType.MESH,
        )

    def start(self):
        pl.when(self.sends)(lambda: self.copy().start())
        self.net.started.append(self)

    def arrived(self):
        pl.when(self.gets)(lambda: self.copy().wait_recv())

    def sent(self):
        pl.when(self.sends)(lambda: self.copy().wait_send())


class Net:
    def __init__(self, size, send_sem, recv_sem):
        self.size = size
        self.place = {axis: lax.axis_index(axis) for axis in size}
        self.send_sem, self.recv_sem = send_sem, recv_sem
        self.used = 0
        self.started = []

    def slot(self):
        self.used += 1
        return self.used - 1

    def target(self, axis, index):
        return tuple(index if name == axis else self.place[name] for name in self.size)

    def bits(self):
        out = []
        for axis, count in self.size.items():
            bit = 1
            while bit < count:
                value = (self.place[axis] // bit) % 2
                out.append((axis, self.place[axis] + bit * (1 - 2 * value), value))
                bit *= 2
        return out

    def greet(self, partners):
        barrier = pltpu.get_barrier_semaphore()
        expected = jnp.int32(0)
        for axis, count in self.size.items():
            here = self.place[axis]
            for delta, there in ((-1, here > 0), (1, here < count - 1)):
                target = self.target(axis, here + delta)

                @pl.when(there)
                def _(target=target):
                    pl.semaphore_signal(
                        barrier, inc=1, device_id=target, device_id_type=pl.DeviceIdType.MESH
                    )

                expected += there.astype(jnp.int32)
        for axis, other, _ in partners:
            pl.semaphore_signal(
                barrier,
                inc=1,
                device_id=self.target(axis, other),
                device_id_type=pl.DeviceIdType.MESH,
            )
        pl.semaphore_wait(barrier, expected + len(partners))

    def finish(self):
        for shift in self.started:
            shift.sent()


def halo(net, ext_ref, margin, between):
    rows, columns = ext_ref.shape[1] - 2 * margin, ext_ref.shape[2] - 2 * margin
    tall, broad = pl.ds(margin, rows), pl.ds(margin, columns)
    near, far = {}, {}
    for axis_name, extent in (("ty", rows), ("tx", columns)):
        near[axis_name] = {-1: pl.ds(margin, margin), 1: pl.ds(extent, margin)}
        far[axis_name] = {-1: pl.ds(extent + margin, margin), 1: pl.ds(0, margin)}
    side = []
    for delta in (-1, 1):
        src = ext_ref.at[:, tall, near["tx"][delta]]
        side.append(Shift(net, src, ext_ref.at[:, tall, far["tx"][delta]], "tx", delta))
    upright = []
    for delta in (-1, 1):
        src = ext_ref.at[:, near["ty"][delta], broad]
        upright.append(Shift(net, src, ext_ref.at[:, far["ty"][delta], broad], "ty", delta))
    for shift in side + upright:
        shift.start()
    between()
    for shift, lanes in zip(side, (pl.ds(columns + margin, margin), pl.ds(0, margin))):
        shift.arrived()
        for delta in (-1, 1):
            src = ext_ref.at[:, near["ty"][delta], lanes]
            dst = ext_ref.at[:, far["ty"][delta], lanes]
            corner = Shift(net, src, dst, "ty", delta, also=shift.gets)
            corner.start()
            upright.append(corner)
    between()
    for shift in upright:
        shift.arrived()


def first_halo_kernel(size, margin, specimen_ref, ext_ref, send_sem, recv_sem):
    net = Net(size, send_sem, recv_sem)
    rows, columns = specimen_ref.shape[1:]
    ext_ref[:, margin : margin + rows, margin : margin + columns] = specimen_ref[...]
    net.greet([])
    halo(net, ext_ref, margin, lambda: None)
    net.finish()


def reduce_steps(net, partners, grads_ref, acc_ref, whole_ref, inbox_refs):
    low, height = 0, grads_ref.shape[1]
    held = grads_ref
    undo = []
    for step, (axis, other, value) in enumerate(partners):
        half = height // 2
        halving = half % SUBLANES == 0
        kept, sent = low, low
        if halving:
            kept = pl.multiple_of(low + value * half, SUBLANES)
            sent = pl.multiple_of(low + (1 - value) * half, SUBLANES)
            height = half
        slot = net.slot()
        inbox = inbox_refs[step]
        source = held.at[:, pl.ds(sent, height), :]
        if not halving:
            outbox = inbox.at[1]
            outbox[...] = held[:, pl.ds(kept, height), :]
            source, inbox = outbox, inbox.at[0]
        copy = pltpu.make_async_remote_copy(
            src_ref=source,
            dst_ref=inbox,
            send_sem=net.send_sem.at[slot],
            recv_sem=net.recv_sem.at[slot],
            device_id=net.target(axis, other),
            device_id_type=pl.DeviceIdType.MESH,
        )
        copy.start()
        yield
        copy.wait()
        acc_ref[:, pl.ds(kept, height), :] = held[:, pl.ds(kept, height), :] + inbox[...]
        held = acc_ref
        if halving:
            undo.append((axis, other, kept, height, low))
        low = kept
    whole_ref[:, pl.ds(low, height), :] = acc_ref[:, pl.ds(low, height), :]
    for axis, other, kept, height, _ in reversed(undo):
        slot = net.slot()
        part = whole_ref.at[:, pl.ds(kept, height), :]
        copy = pltpu.make_async_remote_copy(
            src_ref=part,
            dst_ref=part,
            send_sem=net.send_sem.at[slot],
            recv_sem=net.recv_sem.at[slot],
            device_id=net.target(axis, other),
            device_id_type=pl.DeviceIdType.MESH,
        )
        copy.start()
        yield
        copy.wait()


def settle_kernel(
    size, margin, last, totals_ref, grads_ref, ext_ref, probe_ref, out_ref, probe_out_ref,
    from_rows_ref, strip_ref, from_columns_ref, acc_ref, whole_ref, *rest,
):
    *inbox_refs, send_sem, recv_sem = rest
    net = Net(size, send_sem, recv_sem)
    partners = net.bits()
    rows, columns = ext_ref.shape[1] - 2 * margin, ext_ref.shape[2] - 2 * margin
    shifts = {}
    up, down = 0, 1
    for where, delta, start in ((down, -1, 0), (up, 1, rows + margin)):
        src = totals_ref.at[:, pl.ds(start, margin), :]
        shifts["rows", where] = Shift(net, src, from_rows_ref.at[where], "ty", delta)
    bands = ((0, margin), (margin, rows - 2 * margin), (rows - margin, margin))
    for band, (first, height) in enumerate(bands):
        for where, delta, start in ((1, -1, 0), (0, 1, columns + margin)):
            lanes = pl.ds(start, margin)
            if band == 1:
                src = totals_ref.at[:, pl.ds(margin + first, height), lanes]
            else:
                src = strip_ref.at[band // 2, :, :, lanes]
            dst = from_columns_ref.at[where, :, pl.ds(first, height), :]
            shifts["columns", band, where] = Shift(net, src, dst, "tx", delta)
    for key, ref, axis in (
        ((up, down), from_rows_ref, "ty"),
        ((0, 1), from_columns_ref, "tx"),
    ):
        for where in key:
            missing = net.place[axis] == (0 if where == 0 else size[axis] - 1)

            @pl.when(missing)
            def _(ref=ref, where=where):
                ref[where] = jnp.zeros(ref.shape[1:], jnp.float32)

    net.greet(partners)
    reducing = reduce_steps(net, partners, grads_ref, acc_ref, whole_ref, inbox_refs)

    def step():
        next(reducing, None)

    for where in (up, down):
        shifts["rows", where].start()
    for where in (0, 1):
        shifts["columns", 1, where].start()
    step()
    shift_out = 0 if last else margin

    def renew(band, side):
        first, height = bands[band]
        left, wide = ((0, margin), (margin, columns - 2 * margin), (columns - margin, margin))[side]
        if band == 1:
            total = totals_ref[:, pl.ds(margin + first, height), pl.ds(margin + left, wide)]
        else:
            total = strip_ref[band // 2, :, :, pl.ds(margin + left, wide)]
        if side != 1:
            total = total + from_columns_ref[side // 2, :, pl.ds(first, height), :]
        old = ext_ref[:, pl.ds(margin + first, height), pl.ds(margin + left, wide)]
        new = old + total[:2] / (total[2:] + SPECIMEN_REG)
        out_ref[:, pl.ds(shift_out + first, height), pl.ds(shift_out + left, wide)] = new

    renew(1, 1)
    step()
    for where, start in ((up, margin), (down, rows)):
        shifts["rows", where].arrived()
        strip_ref[where] = totals_ref[:, pl.ds(start, margin), :] + from_rows_ref[where]
        for side in (0, 1):
            shifts["columns", 2 * where, side].start()
    step()
    renew(0, 1)
    renew(2, 1)
    step()
    for band in (1, 0, 2):
        for side in (0, 1):
            shifts["columns", band, side].arrived()
            renew(band, 2 * side)
        step()
    if not last:
        def between():
            step()
            step()

        halo(net, out_ref, margin, between)
    for _ in reducing:
        pass
    whole = whole_ref[...]
    probe_out_ref[...] = probe_ref[...] + whole[:2] / (whole[2:] + PROBE_REG)
    net.finish()


VMEM = pl.BlockSpec(memory_space=pltpu.VMEM)
ROOM = 48 * 1024 * 1024


def first_halo(size, specimen, margin):
    planes, rows, columns = specimen.shape
    return pl.pallas_call(
        functools.partial(first_halo_kernel, size, margin),
        out_shape=jax.ShapeDtypeStruct(
            (planes, rows + 2 * margin, columns + 2 * margin), jnp.float32
        ),
        in_specs=[VMEM],
        out_specs=VMEM,
        scratch_shapes=[pltpu.SemaphoreType.DMA((8,)), pltpu.SemaphoreType.DMA((8,))],
        compiler_params=pltpu.CompilerParams(
            collective_id=0, has_side_effects=True, vmem_limit_bytes=ROOM
        ),
        name="first_halo",
    )(specimen)


def settle(size, totals, grads, extended, probe_field, margin, last):
    window = probe_field.shape[1]
    wide = extended.shape[2]
    rows, columns = extended.shape[1] - 2 * margin, wide - 2 * margin
    inboxes = []
    height = window
    copies = 16
    for count in size.values():
        for _ in range(int(math.log2(count))):
            if (height // 2) % SUBLANES == 0:
                height //= 2
                inboxes.append(pltpu.VMEM((3, height, window), jnp.float32))
            else:
                inboxes.append(pltpu.VMEM((2, 3, height, window), jnp.float32))
            copies += 2
    out = (2, rows, columns) if last else extended.shape
    return pl.pallas_call(
        functools.partial(settle_kernel, size, margin, last),
        out_shape=(
            jax.ShapeDtypeStruct(out, jnp.float32),
            jax.ShapeDtypeStruct(probe_field.shape, jnp.float32),
        ),
        in_specs=[VMEM] * 4,
        out_specs=(VMEM, VMEM),
        scratch_shapes=[
            pltpu.VMEM((2, 3, margin, wide), jnp.float32),
            pltpu.VMEM((2, 3, margin, wide), jnp.float32),
            pltpu.VMEM((2, 3, rows, margin), jnp.float32),
            pltpu.VMEM(grads.shape, jnp.float32),
            pltpu.VMEM(grads.shape, jnp.float32),
            *inboxes,
            pltpu.SemaphoreType.DMA((copies,)),
            pltpu.SemaphoreType.DMA((copies,)),
        ],
        compiler_params=pltpu.CompilerParams(
            collective_id=2 if last else 1, has_side_effects=True, vmem_limit_bytes=ROOM
        ),
        name="settle_last" if last else "settle",
    )(totals, grads, extended, probe_field)


def body(size, specimen, probe_field, intensity, positions, occupied_slots):
    tile_rows = specimen.shape[1]
    tile_columns = specimen.shape[2]
    window = probe_field.shape[1]
    margin = window // 2
    row_start = lax.axis_index("ty") * tile_rows - margin
    column_start = lax.axis_index("tx") * tile_columns - margin
    corners = positions - jnp.stack([row_start, column_start])[None, :]
    extended = first_halo(size, specimen, margin)
    for iteration in range(ITERS):
        totals, grads = sweep(corners, occupied_slots, extended, probe_field, intensity)
        extended, probe_field = settle(
            size, totals, grads, extended, probe_field, margin, iteration == ITERS - 1
        )
    return (extended, probe_field)


def solution(mesh):
    return jax.shard_map(
        functools.partial(body, dict(mesh.shape)),
        mesh=mesh,
        in_specs=(
            P(None, "ty", "tx"),
            P(),
            P(("ty", "tx"), None, None),
            P(("ty", "tx"), None),
            P(("ty", "tx")),
        ),
        out_specs=(P(None, "ty", "tx"), P()),
        check_vma=False,
    )
```

time: 954 us -> 214 us (0.22)
  waiting for transfers between devices: 330 us -> 0 us
  local copies, waits for them, and re-layouts: 248 us -> 4.64 us
  Pallas kernels: 0 us -> 206 us
  matrix products: 157 us -> 0 us
  other arithmetic: 70.6 us -> 0.08 us
  loops' own time: 62.5 us -> 0 us
  starting transfers between devices: 61.9 us -> 0 us
  between operations: 14.9 us -> 0.76 us
    psum x2 -> x0, waiting for transfers between devices: 256 us -> none  [body(): lax.psum((probe_grad, probe_density), ('ty', 'tx'))]
    pallas_call x0 -> x5, Pallas kernels: none -> 206 us  [the longest x2 165 us: settle(): pl.pallas_call(functools.partial(settle_kernel, size, margin, last), out_...]
    dot_general x32 -> x0, matrix products: 157 us -> none  [the longest x16 83.8 us: apply_right(): jnp.einsum('pjk,kl->pjl', batch, matrix, precision=lax.Precision.HIGHEST)]
    dynamic_update_slice x16 -> x0, local copies, waits for them, and re-layouts: 139 us -> none  [deposit(): lax.dynamic_update_slice(running, region + contribution[slot], (anchor, s...]
    ppermute x16 -> x0, waiting for transfers between devices: 73.4 us -> none  [the longest x8 41.2 us: from_behind(): return lax.ppermute(value, axis, pairs)]
    gather x48 -> x0, local copies, waits for them, and re-layouts: 65.2 us -> none
    another operation x4 -> x0, loops' own time: 62.5 us -> none  [the longest x2 61.8 us: run_slots(): totals = lax.fori_loop(0, corners.shape[0], deposit, totals)]
    ppermute x16 -> x0, starting transfers between devices: 61.8 us -> none  [the longest x8 30.6 us: from_behind(): return lax.ppermute(value, axis, pairs)]
  transfers between devices with their start and end apart: 18 -> 0, of which waited for: 16 -> 0; matrix products, arithmetic and copies ran while one was open for 3% -> 0% of each run, Pallas kernels for 0% -> 0%
where the time goes in v1:
time: 214 us; the launch traced here: 212 us
  Pallas kernels  206 us (96%)
  local copies, waits for them, and re-layouts  4.64 us (2%)
    pallas_call x2, Pallas kernels, settle(): pl.pallas_call(functools.partial(settle_kernel, size, margin, last), out_...  165 us
    pallas_call x2, Pallas kernels, sweep(): pl.pallas_call(sweep_kernel, out_shape=(jax.ShapeDtypeStruct((3, rows, co...  21.4 us
    pallas_call x1, Pallas kernels, first_halo(): pl.pallas_call(functools.partial(first_halo_kernel, size, margin), out_sh...  20.1 us
    unnamed x21, local copies, waits for them, and re-layouts  4.64 us

profile of v1, /device:TPU:0, one launch (start us, length us, event | category | flops | bytes accessed | tf_op | source)
XLA Modules:
  0.0 211.6 jit_solution(9927024432016866186)
XLA Ops:
  0.6 0.0 copy-start.1
  0.6 0.0 copy-start
  0.7 0.0 copy-start.2
  0.7 0.1 pad_add_fusion
  0.7 0.9 copy.19
  1.7 0.0 copy-start.3
  1.7 1.6 copy-done.3
  3.2 0.0 copy-start.4
  3.3 0.0 copy-start.8
  3.3 20.1 %first_halo.1.ext_ref = f32[2,768,768]{2,1,0:T(8,128)} custom-call(f32[2,512,512]{2,1,0:T(8,128)S(1)} %copy-done.3), custom_call_target="tpu_custom_call" | custom-call | tf_op jit(solution)/shard_map/first_halo/pallas_call | solution.py:500
  23.4 0.0 copy-done.1
  23.4 0.0 copy-done
  23.4 0.0 copy-done.2
  23.4 0.0 copy-done.4
  23.4 0.0 copy-done.5
  23.5 0.0 copy-done.6
  23.5 0.0 copy-done.7
  23.5 0.0 copy-done.8
  23.5 10.7 %sweep.2 = (f32[3,768,768]{2,1,0:T(8,128)}, f32[3,256,256]{2,1,0:T(8,128)S(1)}) custom-call(s32[8,2]{1,0:T(8,128)S(1)} %broadcast_subtract_fusion.corner_ref, s32[8]{0:T(128)S(1)} %copy-done.8, f32[2,768,768]{2,1,0:T(8,128)} %first_halo.1.ext_ref, f32[2,256,256]{2,1,0:T(8,128)S(1)} %copy-done.2, f32[8,256,256]{2,1,0:T(8,128)S(1)} %copy-done, ...), custom_call_target="tpu_custom_call" | custom-call | tf_op jit(solution)/shard_map/sweep/pallas_call | solution.py:212
  34.2 88.8 %settle.1 = (f32[2,768,768]{2,1,0:T(8,128)}, f32[2,256,256]{2,1,0:T(8,128)S(1)}) custom-call(f32[3,768,768]{2,1,0:T(8,128)} %get-tuple-element.8.totals_ref, f32[3,256,256]{2,1,0:T(8,128)S(1)} %get-tuple-element.9.grads_ref, f32[2,768,768]{2,1,0:T(8,128)} %first_halo.1.ext_ref, f32[2,256,256]{2,1,0:T(8,128)S(1)} %copy-done.2), custom_call_target="tpu_custom_call" | custom-call | tf_op jit(solution)/shard_map/settle/pallas_call | solution.py:531
  123.0 10.7 %sweep.3 = (f32[3,768,768]{2,1,0:T(8,128)}, f32[3,256,256]{2,1,0:T(8,128)S(1)}) custom-call(s32[8,2]{1,0:T(8,128)S(1)} %broadcast_subtract_fusion.corner_ref, s32[8]{0:T(128)S(1)} %copy-done.8, f32[2,768,768]{2,1,0:T(8,128)} %get-tuple-element.10.ext_ref, f32[2,256,256]{2,1,0:T(8,128)S(1)} %get-tuple-element.11.probe_ref, f32[8,256,256]{2,1,0:T(8,128)S(1)} %copy-done, ...), custom_call_target="tpu_custom_call" | custom-call | tf_op jit(solution)/shard_map/sweep/pallas_call | solution.py:212
  133.7 75.8 %settle_last.1 = (f32[2,512,512]{2,1,0:T(8,128)S(1)}, f32[2,256,256]{2,1,0:T(8,128)S(1)}) custom-call(f32[3,768,768]{2,1,0:T(8,128)} %get-tuple-element.12.totals_ref, f32[3,256,256]{2,1,0:T(8,128)S(1)} %get-tuple-element.13.grads_ref, f32[2,768,768]{2,1,0:T(8,128)} %get-tuple-element.10.ext_ref, f32[2,256,256]{2,1,0:T(8,128)S(1)} %get-tuple-element.11.probe_ref), custom_call_target="tpu_custom_call" | custom-call | tf_op jit(solution)/shard_map/settle_last/pallas_call | solution.py:531
  209.5 1.3 copy.22
  210.8 0.8 copy.23
  (4 shorter events, 0.0 us)
Async XLA Ops:
  0.6 22.8 %copy-start.1 = (bf16[256,256]{1,0:T(8,128)(2,1)S(1)}, bf16[256,256]{1,0:T(8,128)(2,1)}, u32[]{:S(2)}) copy-start(bf16[256,256]{1,0:T(8,128)(2,1)} %constant.29.clone.perm_ref.perm_t_ref) | copy-start | bytes 393220
  0.6 22.8 %copy-start = (f32[8,256,256]{2,1,0:T(8,128)S(1)}, f32[8,256,256]{2,1,0:T(8,128)}, u32[]{:S(2)}) copy-start(f32[8,256,256]{2,1,0:T(8,128)} %intensity_ref.3) | copy-start | bytes 6291460
  0.7 22.8 %copy-start.2 = (f32[2,256,256]{2,1,0:T(8,128)S(1)}, f32[2,256,256]{2,1,0:T(8,128)}, u32[]{:S(2)}) copy-start(f32[2,256,256]{2,1,0:T(8,128)} %probe_ref.3) | copy-start | bytes 1572868
  1.7 1.6 copy-start.3
  3.2 20.2 %copy-start.4 = (bf16[768,256]{1,0:T(8,128)(2,1)S(1)}, bf16[768,256]{1,0:T(8,128)(2,1)}, u32[]{:S(2)}) copy-start(bf16[768,256]{1,0:T(8,128)(2,1)} %constant.28.clone.right_t_ref) | copy-start | bytes 1179652
  3.2 20.2 %copy-start.5 = (bf16[256,768]{1,0:T(8,128)(2,1)S(1)}, bf16[256,768]{1,0:T(8,128)(2,1)}, u32[]{:S(2)}) copy-start(bf16[256,768]{1,0:T(8,128)(2,1)} %constant.27.clone.left_t_ref) | copy-start | bytes 1179652
  3.3 20.2 %copy-start.6 = (bf16[768,256]{1,0:T(8,128)(2,1)S(1)}, bf16[768,256]{1,0:T(8,128)(2,1)}, u32[]{:S(2)}) copy-start(bf16[768,256]{1,0:T(8,128)(2,1)} %constant.26.clone.right_ref) | copy-start | bytes 1179652
  3.3 20.2 %copy-start.7 = (bf16[256,768]{1,0:T(8,128)(2,1)S(1)}, bf16[256,768]{1,0:T(8,128)(2,1)}, u32[]{:S(2)}) copy-start(bf16[256,768]{1,0:T(8,128)(2,1)} %constant.25.clone.left_ref) | copy-start | bytes 1179652
  3.3 20.2 %copy-start.8 = (s32[8]{0:T(128)S(1)}, s32[8]{0:T(128)}, u32[]{:S(2)}) copy-start(s32[8]{0:T(128)} %alive_ref.3) | copy-start | bytes 100

commit v2 on v1

--- a/solution.py
+++ b/solution.py
@@ -102,12 +102,12 @@
 
 
 def sweep_kernel(
-    corner_ref, alive_ref, ext_ref, probe_ref, intensity_ref,
-    left_ref, right_ref, left_t_ref, right_t_ref, perm_ref, perm_t_ref,
+    corner_ref, alive_ref, ext_ref, probe_ref, amplitude_ref,
+    left_ref, right_ref, left_t_ref, right_t_ref,
     totals_ref, grad_ref, power_ref,
 ):
     window = probe_ref.shape[1]
-    slots = intensity_ref.shape[0]
+    slots = amplitude_ref.shape[0]
     last_top = ext_ref.shape[1] - window - SUBLANES
     last_start = ext_ref.shape[2] - window - LANES
     totals_ref[...] = jnp.zeros_like(totals_ref)
@@ -177,12 +177,7 @@
             zr, zi = spread(
                 times_right(yr, right_ref[...]), times_right(yi, right_ref[...]), 1
             )
-            amplitude = jnp.sqrt(intensity_ref[slot])
-            hi, mid = split(amplitude)
-            rest = amplitude - hi.astype(jnp.float32) - mid.astype(jnp.float32)
-            low = rest.astype(jnp.bfloat16)
-            rows = [dot(perm_ref[...], part).astype(jnp.bfloat16) for part in (hi, mid, low)]
-            amplitude = sum(dot(part, perm_t_ref[...]) for part in rows)
+            amplitude = amplitude_ref[slot]
             magnitude = jnp.sqrt(zr * zr + zi * zi)
             factor = amplitude / jnp.maximum(magnitude, FLOOR)
             zr, zi = gather_pairs(zr * factor, zi * factor, 0)
@@ -203,12 +198,12 @@
     lax.fori_loop(0, slots, visit, 0)
 
 
-def sweep(corners, occupied, extended, probe_field, intensity):
+def sweep(corners, occupied, extended, probe_field, amplitude):
     window = probe_field.shape[1]
     rows, columns = extended.shape[1:]
     smem = pl.BlockSpec(memory_space=pltpu.SMEM)
     vmem = pl.BlockSpec(memory_space=pltpu.VMEM)
-    consts = [jnp.asarray(t) for t in tables(window)]
+    consts = [jnp.asarray(t) for t in tables(window)[:4]]
     return pl.pallas_call(
         sweep_kernel,
         out_shape=(
@@ -220,7 +215,7 @@
         scratch_shapes=[pltpu.VMEM((window, window), jnp.float32)],
         compiler_params=pltpu.CompilerParams(vmem_limit_bytes=48 * 1024 * 1024),
         name="sweep",
-    )(corners, occupied, extended, probe_field, intensity, *consts)
+    )(corners, occupied, extended, probe_field, amplitude, *consts)
 
 
 class Shift:
@@ -279,7 +274,9 @@
                 value = (self.place[axis] // bit) % 2
                 out.append((axis, self.place[axis] + bit * (1 - 2 * value), value))
                 bit *= 2
-        return out
+        rows = [entry for entry in out if entry[0] == "ty"]
+        columns = [entry for entry in out if entry[0] == "tx"]
+        return rows[:1] + rows[:1:-1] + columns + rows[1:2]
 
     def greet(self, partners):
         barrier = pltpu.get_barrier_semaphore()
@@ -341,12 +338,30 @@
         shift.arrived()
 
 
-def first_halo_kernel(size, margin, specimen_ref, ext_ref, send_sem, recv_sem):
+def first_halo_kernel(
+    size, margin, specimen_ref, intensity_ref, perm_ref, perm_t_ref, ext_ref, amplitude_ref,
+    send_sem, recv_sem,
+):
     net = Net(size, send_sem, recv_sem)
     rows, columns = specimen_ref.shape[1:]
     ext_ref[:, margin : margin + rows, margin : margin + columns] = specimen_ref[...]
     net.greet([])
-    halo(net, ext_ref, margin, lambda: None)
+
+    def order(first, last):
+        def visit(slot, carry):
+            amplitude = jnp.sqrt(intensity_ref[slot])
+            hi, mid = split(amplitude)
+            rest = amplitude - hi.astype(jnp.float32) - mid.astype(jnp.float32)
+            low = rest.astype(jnp.bfloat16)
+            rows = [dot(perm_ref[...], part).astype(jnp.bfloat16) for part in (hi, mid, low)]
+            amplitude_ref[slot] = sum(dot(part, perm_t_ref[...]) for part in rows)
+            return carry
+
+        lax.fori_loop(first, last, visit, 0)
+
+    slots = intensity_ref.shape[0]
+    parts = iter([(0, slots - 2), (slots - 2, slots)])
+    halo(net, ext_ref, margin, lambda: order(*next(parts)))
     net.finish()
 
 
@@ -412,9 +427,12 @@
     rows, columns = ext_ref.shape[1] - 2 * margin, ext_ref.shape[2] - 2 * margin
     shifts = {}
     up, down = 0, 1
+    pieces = (pl.ds(0, margin), pl.ds(columns + margin, margin), pl.ds(margin, columns))
     for where, delta, start in ((down, -1, 0), (up, 1, rows + margin)):
-        src = totals_ref.at[:, pl.ds(start, margin), :]
-        shifts["rows", where] = Shift(net, src, from_rows_ref.at[where], "ty", delta)
+        for piece, lanes in enumerate(pieces):
+            src = totals_ref.at[:, pl.ds(start, margin), lanes]
+            dst = from_rows_ref.at[where, :, :, lanes]
+            shifts["rows", where, piece] = Shift(net, src, dst, "ty", delta)
     bands = ((0, margin), (margin, rows - 2 * margin), (rows - margin, margin))
     for band, (first, height) in enumerate(bands):
         for where, delta, start in ((1, -1, 0), (0, 1, columns + margin)):
@@ -442,11 +460,14 @@
     def step():
         next(reducing, None)
 
-    for where in (up, down):
-        shifts["rows", where].start()
+    for piece in (0, 1):
+        for where in (up, down):
+            shifts["rows", where, piece].start()
+    step()
     for where in (0, 1):
         shifts["columns", 1, where].start()
-    step()
+    for where in (up, down):
+        shifts["rows", where, 2].start()
     shift_out = 0 if last else margin
 
     def renew(band, side):
@@ -462,17 +483,27 @@
         new = old + total[:2] / (total[2:] + SPECIMEN_REG)
         out_ref[:, pl.ds(shift_out + first, height), pl.ds(shift_out + left, wide)] = new
 
+    def join(where, piece):
+        lanes = pieces[piece]
+        start = margin if where == up else rows
+        shifts["rows", where, piece].arrived()
+        strip_ref[where, :, :, lanes] = (
+            totals_ref[:, pl.ds(start, margin), lanes] + from_rows_ref[where, :, :, lanes]
+        )
+
+    step()
     renew(1, 1)
     step()
-    for where, start in ((up, margin), (down, rows)):
-        shifts["rows", where].arrived()
-        strip_ref[where] = totals_ref[:, pl.ds(start, margin), :] + from_rows_ref[where]
-        for side in (0, 1):
-            shifts["columns", 2 * where, side].start()
+    for side in (0, 1):
+        for where in (up, down):
+            join(where, side)
+            shifts["columns", 2 * where, 1 - side].start()
     step()
-    renew(0, 1)
-    renew(2, 1)
     step()
+    for where in (up, down):
+        join(where, 2)
+        renew(2 * where, 1)
+        step()
     for band in (1, 0, 2):
         for side in (0, 1):
             shifts["columns", band, side].arrived()
@@ -495,21 +526,22 @@
 ROOM = 48 * 1024 * 1024
 
 
-def first_halo(size, specimen, margin):
+def first_halo(size, specimen, intensity, margin):
     planes, rows, columns = specimen.shape
     return pl.pallas_call(
         functools.partial(first_halo_kernel, size, margin),
-        out_shape=jax.ShapeDtypeStruct(
-            (planes, rows + 2 * margin, columns + 2 * margin), jnp.float32
+        out_shape=(
+            jax.ShapeDtypeStruct((planes, rows + 2 * margin, columns + 2 * margin), jnp.float32),
+            jax.ShapeDtypeStruct(intensity.shape, jnp.float32),
         ),
-        in_specs=[VMEM],
-        out_specs=VMEM,
+        in_specs=[VMEM] * 4,
+        out_specs=(VMEM, VMEM),
         scratch_shapes=[pltpu.SemaphoreType.DMA((8,)), pltpu.SemaphoreType.DMA((8,))],
         compiler_params=pltpu.CompilerParams(
             collective_id=0, has_side_effects=True, vmem_limit_bytes=ROOM
         ),
         name="first_halo",
-    )(specimen)
+    )(specimen, intensity, *[jnp.asarray(t) for t in tables(intensity.shape[1])[4:]])
 
 
 def settle(size, totals, grads, extended, probe_field, margin, last):
@@ -518,7 +550,7 @@
     rows, columns = extended.shape[1] - 2 * margin, wide - 2 * margin
     inboxes = []
     height = window
-    copies = 16
+    copies = 20
     for count in size.values():
         for _ in range(int(math.log2(count))):
             if (height // 2) % SUBLANES == 0:
@@ -561,9 +593,9 @@
     row_start = lax.axis_index("ty") * tile_rows - margin
     column_start = lax.axis_index("tx") * tile_columns - margin
     corners = positions - jnp.stack([row_start, column_start])[None, :]
-    extended = first_halo(size, specimen, margin)
+    extended, amplitude = first_halo(size, specimen, intensity, margin)
     for iteration in range(ITERS):
-        totals, grads = sweep(corners, occupied_slots, extended, probe_field, intensity)
+        totals, grads = sweep(corners, occupied_slots, extended, probe_field, amplitude)
         extended, probe_field = settle(
             size, totals, grads, extended, probe_field, margin, iteration == ITERS - 1
         )

time: 214 us -> 197 us (0.921)
  Pallas kernels: 206 us -> 190 us
    pallas_call x2, Pallas kernels: 165 us -> 139 us  [settle(): pl.pallas_call(functools.partial(settle_kernel, size, margin, last), out_...]
    pallas_call x2, Pallas kernels: 21.4 us -> 29.4 us  [sweep(): pl.pallas_call(sweep_kernel, out_shape=(jax.ShapeDtypeStruct((3, rows, co...]
    unnamed x21 -> x19, local copies, waits for them, and re-layouts: 4.64 us -> 5.39 us
where the time goes in v2:
time: 197 us
  Pallas kernels  190 us (96%)
  local copies, waits for them, and re-layouts  5.39 us (3%)
    pallas_call x2, Pallas kernels, settle(): pl.pallas_call(functools.partial(settle_kernel, size, margin, last), out_...  139 us
    pallas_call x2, Pallas kernels, sweep(): pl.pallas_call(sweep_kernel, out_shape=(jax.ShapeDtypeStruct((3, rows, co...  29.4 us
    pallas_call x1, Pallas kernels, first_halo(): pl.pallas_call(functools.partial(first_halo_kernel, size, margin), out_sh...  22.1 us
    unnamed x19, local copies, waits for them, and re-layouts  5.39 us

profile of v2, /device:TPU:0, one launch (start us, length us, event | category | flops | bytes accessed | tf_op | source)
XLA Modules:
  0.0 196.7 jit_solution(48075666775439014)
XLA Ops:
  0.6 0.1 pad_add_fusion
  0.7 0.8 copy.17
  1.5 0.0 copy-start.1
  1.5 1.6 copy-done.1
  3.1 0.0 copy-start.6
  3.1 0.9 copy-done.6
  4.0 0.0 copy-start
  4.0 0.0 copy-start.2
  4.0 0.0 copy-start.4
  4.0 0.0 copy-start.5
  4.0 0.0 copy-start.7
  4.0 22.1 %first_halo.1 = (f32[2,768,768]{2,1,0:T(8,128)}, f32[8,256,256]{2,1,0:T(8,128)S(1)}) custom-call(f32[2,512,512]{2,1,0:T(8,128)S(1)} %copy-done.1, f32[8,256,256]{2,1,0:T(8,128)} %intensity_ref.1, bf16[256,256]{1,0:T(8,128)(2,1)S(1)} %copy-done.6, bf16[256,256]{1,0:T(8,128)(2,1)S(1)} %copy-done.6), custom_call_target="tpu_custom_call" | custom-call | tf_op jit(solution)/shard_map/first_halo/pallas_call | solution.py:531
  26.1 0.0 copy-done
  26.1 0.0 copy-done.2
  26.1 0.0 copy-done.3
  26.1 0.0 copy-done.4
  26.1 0.0 copy-done.5
  26.1 0.0 copy-done.7
  26.1 14.7 %sweep.2 = (f32[3,768,768]{2,1,0:T(8,128)}, f32[3,256,256]{2,1,0:T(8,128)S(1)}) custom-call(s32[8,2]{1,0:T(8,128)S(1)} %broadcast_subtract_fusion.corner_ref, s32[8]{0:T(128)S(1)} %copy-done.7, f32[2,768,768]{2,1,0:T(8,128)} %get-tuple-element.10.ext_ref, f32[2,256,256]{2,1,0:T(8,128)S(1)} %copy-done, f32[8,256,256]{2,1,0:T(8,128)S(1)} %get-tuple-element.11.amplitude_ref, ...), custom_call_target="tpu_custom_call" | custom-call | tf_op jit(solution)/shard_map/sweep/pallas_call | solution.py:207
  40.8 75.8 %settle.1 = (f32[2,768,768]{2,1,0:T(8,128)}, f32[2,256,256]{2,1,0:T(8,128)S(1)}) custom-call(f32[3,768,768]{2,1,0:T(8,128)} %get-tuple-element.12.totals_ref, f32[3,256,256]{2,1,0:T(8,128)S(1)} %get-tuple-element.13.grads_ref, f32[2,768,768]{2,1,0:T(8,128)} %get-tuple-element.10.ext_ref, f32[2,256,256]{2,1,0:T(8,128)S(1)} %copy-done), custom_call_target="tpu_custom_call" | custom-call | tf_op jit(solution)/shard_map/settle/pallas_call | solution.py:563
  116.6 14.7 %sweep.3 = (f32[3,768,768]{2,1,0:T(8,128)}, f32[3,256,256]{2,1,0:T(8,128)S(1)}) custom-call(s32[8,2]{1,0:T(8,128)S(1)} %broadcast_subtract_fusion.corner_ref, s32[8]{0:T(128)S(1)} %copy-done.7, f32[2,768,768]{2,1,0:T(8,128)} %get-tuple-element.14.ext_ref, f32[2,256,256]{2,1,0:T(8,128)S(1)} %get-tuple-element.15.probe_ref, ...), custom_call_target="tpu_custom_call" | custom-call | tf_op jit(solution)/shard_map/sweep/pallas_call | solution.py:207
  131.3 63.2 %settle_last.1 = (f32[2,512,512]{2,1,0:T(8,128)S(1)}, f32[2,256,256]{2,1,0:T(8,128)S(1)}) custom-call(f32[3,768,768]{2,1,0:T(8,128)} %get-tuple-element.16.totals_ref, f32[3,256,256]{2,1,0:T(8,128)S(1)} %get-tuple-element.17.grads_ref, f32[2,768,768]{2,1,0:T(8,128)} %get-tuple-element.14.ext_ref, f32[2,256,256]{2,1,0:T(8,128)S(1)} %get-tuple-element.15.probe_ref), custom_call_target="tpu_custom_call" | custom-call | tf_op jit(solution)/shard_map/settle_last/pallas_call | solution.py:563
  194.5 1.3 copy.20
  195.9 0.8 copy.21
  (2 shorter events, 0.0 us)
Async XLA Ops:
  1.5 1.6 copy-start.1
  3.1 0.9 copy-start.6
  4.0 22.1 %copy-start = (f32[2,256,256]{2,1,0:T(8,128)S(1)}, f32[2,256,256]{2,1,0:T(8,128)}, u32[]{:S(2)}) copy-start(f32[2,256,256]{2,1,0:T(8,128)} %probe_ref.3) | copy-start | bytes 1572868
  4.0 22.1 %copy-start.2 = (bf16[768,256]{1,0:T(8,128)(2,1)S(1)}, bf16[768,256]{1,0:T(8,128)(2,1)}, u32[]{:S(2)}) copy-start(bf16[768,256]{1,0:T(8,128)(2,1)} %constant.29.clone.right_t_ref) | copy-start | bytes 1179652
  4.0 22.1 %copy-start.3 = (bf16[256,768]{1,0:T(8,128)(2,1)S(1)}, bf16[256,768]{1,0:T(8,128)(2,1)}, u32[]{:S(2)}) copy-start(bf16[256,768]{1,0:T(8,128)(2,1)} %constant.28.clone.left_t_ref) | copy-start | bytes 1179652
  4.0 22.1 %copy-start.4 = (bf16[768,256]{1,0:T(8,128)(2,1)S(1)}, bf16[768,256]{1,0:T(8,128)(2,1)}, u32[]{:S(2)}) copy-start(bf16[768,256]{1,0:T(8,128)(2,1)} %constant.27.clone.right_ref) | copy-start | bytes 1179652
  4.0 22.1 %copy-start.5 = (bf16[256,768]{1,0:T(8,128)(2,1)S(1)}, bf16[256,768]{1,0:T(8,128)(2,1)}, u32[]{:S(2)}) copy-start(bf16[256,768]{1,0:T(8,128)(2,1)} %constant.26.clone.left_ref) | copy-start | bytes 1179652
  4.0 22.1 %copy-start.7 = (s32[8]{0:T(128)S(1)}, s32[8]{0:T(128)}, u32[]{:S(2)}) copy-start(s32[8]{0:T(128)} %alive_ref.3) | copy-start | bytes 100

commit v3 on v2

--- a/solution.py
+++ b/solution.py
@@ -213,7 +213,7 @@
         in_specs=[smem, smem] + [vmem] * (3 + len(consts)),
         out_specs=(vmem, vmem),
         scratch_shapes=[pltpu.VMEM((window, window), jnp.float32)],
-        compiler_params=pltpu.CompilerParams(vmem_limit_bytes=48 * 1024 * 1024),
+        compiler_params=pltpu.CompilerParams(vmem_limit_bytes=32 * 1024 * 1024),
         name="sweep",
     )(corners, occupied, extended, probe_field, amplitude, *consts)
 
@@ -523,7 +523,7 @@
 
 
 VMEM = pl.BlockSpec(memory_space=pltpu.VMEM)
-ROOM = 48 * 1024 * 1024
+ROOM = 32 * 1024 * 1024
 
 
 def first_halo(size, specimen, intensity, margin):

time: 197 us -> 183 us (0.929)
  Pallas kernels: 190 us -> 162 us
  local copies, waits for them, and re-layouts: 5.39 us -> 18.7 us
    pallas_call x2, Pallas kernels: 29.4 us -> 15.6 us  [sweep(): pl.pallas_call(sweep_kernel, out_shape=(jax.ShapeDtypeStruct((3, rows, co...]
    unnamed x19 -> x29, local copies, waits for them, and re-layouts: 5.39 us -> 18.7 us
    pallas_call x2, Pallas kernels: 139 us -> 129 us  [settle(): pl.pallas_call(functools.partial(settle_kernel, size, margin, last), out_...]
    pallas_call x1, Pallas kernels: 22.1 us -> 18.2 us  [first_halo(): pl.pallas_call(functools.partial(first_halo_kernel, size, margin), out_sh...]
where the time goes in v3:
time: 183 us; the launch traced here: 182 us
  Pallas kernels  162 us (89%)
  local copies, waits for them, and re-layouts  18.7 us (10%)
    pallas_call x2, Pallas kernels, settle(): pl.pallas_call(functools.partial(settle_kernel, size, margin, last), out_...  129 us
    unnamed x29, local copies, waits for them, and re-layouts  18.7 us
    pallas_call x1, Pallas kernels, first_halo(): pl.pallas_call(functools.partial(first_halo_kernel, size, margin), out_sh...  18.2 us
    pallas_call x2, Pallas kernels, sweep(): pl.pallas_call(sweep_kernel, out_shape=(jax.ShapeDtypeStruct((3, rows, co...  15.6 us

profile of v3, /device:TPU:0, one launch (start us, length us, event | category | flops | bytes accessed | tf_op | source)
XLA Modules:
  0.0 182.0 jit_solution(8604912281616779818)
XLA Ops:
  0.6 0.1 pad_add_fusion
  0.7 0.8 copy.17
  1.5 1.6 copy-done.5
  3.1 1.6 copy-done.6
  4.7 0.9 copy-done.11
  5.6 0.0 copy-start.10
  5.6 0.0 copy-start.12
  5.6 18.2 %first_halo.1 = (f32[2,768,768]{2,1,0:T(8,128)S(1)}, f32[8,256,256]{2,1,0:T(8,128)S(1)}) custom-call(f32[2,512,512]{2,1,0:T(8,128)S(1)} %copy-done.5, f32[8,256,256]{2,1,0:T(8,128)S(1)} %copy-done.6, bf16[256,256]{1,0:T(8,128)(2,1)S(1)} %copy-done.11, bf16[256,256]{1,0:T(8,128)(2,1)S(1)} %copy-done.11), custom_call_target="tpu_custom_call" | custom-call | tf_op jit(solution)/shard_map/first_halo/pallas_call | solution.py:531
  23.8 0.0 copy-done.4
  23.8 0.0 copy-done.7
  23.8 0.0 copy-done.8
  23.8 0.0 copy-done.9
  23.8 0.0 copy-done.10
  23.8 0.0 copy-done.12
  23.8 7.8 %sweep.2 = (f32[3,768,768]{2,1,0:T(8,128)S(1)}, f32[3,256,256]{2,1,0:T(8,128)S(1)}) custom-call(s32[8,2]{1,0:T(8,128)S(1)} %broadcast_subtract_fusion.corner_ref, s32[8]{0:T(128)S(1)} %copy-done.12, f32[2,768,768]{2,1,0:T(8,128)S(1)} %get-tuple-element.10.ext_ref, f32[2,256,256]{2,1,0:T(8,128)S(1)} %copy-done.4, ...), custom_call_target="tpu_custom_call" | custom-call | tf_op jit(solution)/shard_map/sweep/pallas_call | solution.py:207
  31.6 2.9 %copy-done.2 = f32[3,768,768]{2,1,0:T(8,128)} copy-done((f32[3,768,768]{2,1,0:T(8,128)}, f32[3,768,768]{2,1,0:T(8,128)S(1)}, u32[]{:S(2)}) %copy-start.2) | copy-done | bytes 7077912
  34.5 3.0 %copy-done.3 = f32[3,768,768]{2,1,0:T(8,128)S(1)} copy-done((f32[3,768,768]{2,1,0:T(8,128)S(1)}, f32[3,768,768]{2,1,0:T(8,128)}, u32[]{:S(2)}) %copy-start.3) | copy-done | bytes 7077912
  37.5 71.0 %settle.1 = (f32[2,768,768]{2,1,0:T(8,128)S(1)}, f32[2,256,256]{2,1,0:T(8,128)S(1)}) custom-call(f32[3,768,768]{2,1,0:T(8,128)S(1)} %copy-done.3, f32[3,256,256]{2,1,0:T(8,128)S(1)} %get-tuple-element.13.grads_ref, f32[2,768,768]{2,1,0:T(8,128)S(1)} %get-tuple-element.10.ext_ref, f32[2,256,256]{2,1,0:T(8,128)S(1)} %copy-done.4), custom_call_target="tpu_custom_call" | custom-call | tf_op jit(solution)/shard_map/settle/pallas_call | solution.py:563
  108.6 7.8 %sweep.3 = (f32[3,768,768]{2,1,0:T(8,128)S(1)}, f32[3,256,256]{2,1,0:T(8,128)S(1)}) custom-call(s32[8,2]{1,0:T(8,128)S(1)} %broadcast_subtract_fusion.corner_ref, s32[8]{0:T(128)S(1)} %copy-done.12, f32[2,768,768]{2,1,0:T(8,128)S(1)} %get-tuple-element.14.ext_ref, f32[2,256,256]{2,1,0:T(8,128)S(1)} %get-tuple-element.15.probe_ref, ...), custom_call_target="tpu_custom_call" | custom-call | tf_op jit(solution)/shard_map/sweep/pallas_call | solution.py:207
  116.4 2.9 %copy-done = f32[3,768,768]{2,1,0:T(8,128)} copy-done((f32[3,768,768]{2,1,0:T(8,128)}, f32[3,768,768]{2,1,0:T(8,128)S(1)}, u32[]{:S(2)}) %copy-start) | copy-done | bytes 7077912
  119.2 3.0 %copy-done.1 = f32[3,768,768]{2,1,0:T(8,128)S(1)} copy-done((f32[3,768,768]{2,1,0:T(8,128)S(1)}, f32[3,768,768]{2,1,0:T(8,128)}, u32[]{:S(2)}) %copy-start.1) | copy-done | bytes 7077912
  122.3 57.6 %settle_last.1 = (f32[2,512,512]{2,1,0:T(8,128)S(1)}, f32[2,256,256]{2,1,0:T(8,128)S(1)}) custom-call(f32[3,768,768]{2,1,0:T(8,128)S(1)} %copy-done.1, f32[3,256,256]{2,1,0:T(8,128)S(1)} %get-tuple-element.17.grads_ref, f32[2,768,768]{2,1,0:T(8,128)S(1)} %get-tuple-element.14.ext_ref, f32[2,256,256]{2,1,0:T(8,128)S(1)} %get-tuple-element.15.probe_ref), custom_call_target="tpu_custom_call" | custom-call | tf_op jit(solution)/shard_map/settle_last/pallas_call | solution.py:563
  179.9 1.3 copy.20
  181.2 0.8 copy.21
  (12 shorter events, 0.0 us)
Async XLA Ops:
  1.5 1.6 copy-start.5
  3.1 1.6 copy-start.6
  4.7 0.9 copy-start.11
  5.6 18.2 %copy-start.4 = (f32[2,256,256]{2,1,0:T(8,128)S(1)}, f32[2,256,256]{2,1,0:T(8,128)}, u32[]{:S(2)}) copy-start(f32[2,256,256]{2,1,0:T(8,128)} %probe_ref.3) | copy-start | bytes 1572868
  5.6 18.2 %copy-start.7 = (bf16[768,256]{1,0:T(8,128)(2,1)S(1)}, bf16[768,256]{1,0:T(8,128)(2,1)}, u32[]{:S(2)}) copy-start(bf16[768,256]{1,0:T(8,128)(2,1)} %constant.29.clone.right_t_ref) | copy-start | bytes 1179652
  5.6 18.2 %copy-start.8 = (bf16[256,768]{1,0:T(8,128)(2,1)S(1)}, bf16[256,768]{1,0:T(8,128)(2,1)}, u32[]{:S(2)}) copy-start(bf16[256,768]{1,0:T(8,128)(2,1)} %constant.28.clone.left_t_ref) | copy-start | bytes 1179652
  5.6 18.2 %copy-start.9 = (bf16[768,256]{1,0:T(8,128)(2,1)S(1)}, bf16[768,256]{1,0:T(8,128)(2,1)}, u32[]{:S(2)}) copy-start(bf16[768,256]{1,0:T(8,128)(2,1)} %constant.27.clone.right_ref) | copy-start | bytes 1179652
  5.6 18.2 %copy-start.10 = (bf16[256,768]{1,0:T(8,128)(2,1)S(1)}, bf16[256,768]{1,0:T(8,128)(2,1)}, u32[]{:S(2)}) copy-start(bf16[256,768]{1,0:T(8,128)(2,1)} %constant.26.clone.left_ref) | copy-start | bytes 1179652
  5.6 18.2 %copy-start.12 = (s32[8]{0:T(128)S(1)}, s32[8]{0:T(128)}, u32[]{:S(2)}) copy-start(s32[8]{0:T(128)} %alive_ref.3) | copy-start | bytes 100
  31.6 2.9 %copy-start.2 = (f32[3,768,768]{2,1,0:T(8,128)}, f32[3,768,768]{2,1,0:T(8,128)S(1)}, u32[]{:S(2)}) copy-start(f32[3,768,768]{2,1,0:T(8,128)S(1)} %get-tuple-element.12.totals_ref) | copy-start | bytes 21233668
  34.5 3.0 %copy-start.3 = (f32[3,768,768]{2,1,0:T(8,128)S(1)}, f32[3,768,768]{2,1,0:T(8,128)}, u32[]{:S(2)}) copy-start(f32[3,768,768]{2,1,0:T(8,128)} %copy-done.2) | copy-start | bytes 21233668
  116.4 2.9 %copy-start = (f32[3,768,768]{2,1,0:T(8,128)}, f32[3,768,768]{2,1,0:T(8,128)S(1)}, u32[]{:S(2)}) copy-start(f32[3,768,768]{2,1,0:T(8,128)S(1)} %get-tuple-element.16.totals_ref) | copy-start | bytes 21233668
  119.2 3.0 %copy-start.1 = (f32[3,768,768]{2,1,0:T(8,128)S(1)}, f32[3,768,768]{2,1,0:T(8,128)}, u32[]{:S(2)}) copy-start(f32[3,768,768]{2,1,0:T(8,128)} %copy-done) | copy-start | bytes 21233668
